TPU v7x, 32 devices: a whole 2x2x4 slice. The times are simulated.
32 devices in a mesh: fish: 2 (over y), img: 16 (over z, x, core).
Axes of the slice: x: 2, y: 2, z: 4, core: 2. Of those that a mesh axis runs over, the one named last changes fastest.
Arguments:
- img_feat: bfloat16 [64, 16384], P(None, ('fish', 'img')), parts along dimension 1, may hold values from -80 to 80
- mdl_feat: bfloat16 [64, 2048], P(None, ('fish', 'img')), parts along dimension 1, may hold values from -80 to 80
- img_mass: float32 [16384], P(('fish', 'img')), parts along dimension 0, may hold values from 0.5 to 2
- mdl_mass: float32 [2048], P('fish'), parts along dimension 0, may hold values from 0.5 to 2
Outputs:
- grad_img: float32 [64, 16384], P(None, ('fish', 'img')), parts along dimension 1
- grad_mdl: float32 [64, 2048], P(None, ('fish', 'img')), parts along dimension 1
There are 2 independent parts, one for each index of `fish`. A program takes and returns all parts, laid end to end along the dimension named above; each array names one. Nothing has to cross between parts.
All inputs are finite; a program needn't handle non-finite values.
Results may differ from a plain program's by a relative error of at most 0.005.
Values may be sent and summed in bfloat16 or wider, within the bound.
A program may use at most 64 MiB of HBM per device.

v0:
```python
import jax
import jax.numpy as jnp
from jax import lax
from jax.sharding import PartitionSpec as P

FEAT = 64
ITERS = 4


inv_temp = 20.0


def normalize(features):
    wide = features.astype(jnp.float32)
    guarded = jnp.mean(wide * wide, axis=0, keepdims=True) + 1e-06
    return (wide * lax.rsqrt(guarded)).astype(jnp.bfloat16)


def kernel_tile(imaged_unit, model_slice, factor):
    scores = lax.dot_general(
        imaged_unit, model_slice, (((0,), (0,)), ((), ())), preferred_element_type=jnp.float32
    )
    return jnp.exp(scores * factor).astype(jnp.bfloat16)


def shards(img_feat, mdl_feat, img_mass, mdl_mass):
    factor = inv_temp / FEAT
    imaged_unit = normalize(img_feat)
    model_unit = lax.all_gather(normalize(mdl_feat), "img", axis=1, tiled=True)
    total_model = model_unit.shape[1]
    share = mdl_feat.shape[1]
    local_rows = img_feat.shape[1]
    offset = lax.axis_index("img") * share
    kernel = kernel_tile(imaged_unit, model_unit, factor)
    col_scale = jnp.ones((total_model,), jnp.float32)
    col_low = col_scale.astype(jnp.bfloat16)
    row_scale = jnp.ones((local_rows,), jnp.float32)
    for iteration in range(ITERS):
        row_scale = img_mass / jnp.dot(kernel, col_low, preferred_element_type=jnp.float32)
        partial_cols = jnp.dot(
            row_scale.astype(jnp.bfloat16), kernel, preferred_element_type=jnp.float32
        )
        col_scale = mdl_mass / lax.psum(partial_cols, "img")
        col_low = col_scale.astype(jnp.bfloat16)
    weighted = (model_unit.astype(jnp.float32) * col_scale[None, :]).astype(jnp.bfloat16)
    grad_img = -(
        lax.dot_general(
            weighted, kernel, (((1,), (1,)), ((), ())), preferred_element_type=jnp.float32
        )
        * row_scale[None, :]
    )
    row_feat = (imaged_unit.astype(jnp.float32) * row_scale[None, :]).astype(jnp.bfloat16)
    summed = lax.psum_scatter(
        lax.dot_general(
            kernel, row_feat, (((0,), (1,)), ((), ())), preferred_element_type=jnp.float32
        ),
        "img",
        scatter_dimension=0,
        tiled=True,
    )
    own_scale = lax.dynamic_slice_in_dim(col_scale, offset, share, 0)
    grad_mdl = -(summed * own_scale[:, None]).T
    return (grad_img, grad_mdl)


def solution(mesh):
    placed = (P(None, ("fish", "img")), P(None, ("fish", "img")), P(("fish", "img")), P("fish"))
    return jax.shard_map(
        shards,
        mesh=mesh,
        in_specs=placed,
        out_specs=(P(None, ("fish", "img")), P(None, ("fish", "img"))),
        check_vma=False,
    )
```

profile of v0, /device:TPU:0, one launch (start us, length us, event | category | flops | bytes accessed | tf_op | source)
XLA Modules:
  0.0 188.4 jit_solution(11212692938415362139)
XLA Ops:
  7.2 0.8 copy.7
  8.0 0.1 fusion.8
  8.1 0.1 fusion.9
  8.2 23.8 %all_gather.3 = bf16[64,1024]{0,1:T(8,128)(2,1)S(1)} all-gather(bf16[64,64]{0,1:T(8,128)(2,1)S(1)} %fusion.9), channel_id=1, replica_groups=mesh['fish'=2,'img'=16] {'img'}, dimensions={1}, use_global_device_ids=true | all-gather | bytes 139264 | tf_op jit(solution)/shard_map/all_gather | solution.py:29
  32.0 0.9 fusion.2
  32.9 1.3 exponential_convert_fusion
  34.2 0.4 fusion.10
  34.7 0.2 fusion.14
  34.9 29.8 %psum.28 = f32[1024]{0:T(1024)S(1)} all-reduce(f32[1024]{0:T(1024)S(1)} %bitcast.28), channel_id=1, replica_groups=mesh['fish'=2,'img'=16] {'img'}, use_global_device_ids=true, to_apply=%region_2.0 | all-reduce | flops 1024 | bytes 8192 | tf_op jit(solution)/shard_map/psum | solution.py:43
  64.7 0.4 fusion.15
  65.1 0.3 fusion.16
  65.4 29.5 %psum.29 = f32[1024]{0:T(1024)S(1)} all-reduce(f32[1024]{0:T(1024)S(1)} %bitcast.29), channel_id=1, replica_groups=mesh['fish'=2,'img'=16] {'img'}, use_global_device_ids=true, to_apply=%region_3.0 | all-reduce | flops 1024 | bytes 8192 | tf_op jit(solution)/shard_map/psum | solution.py:43
  94.9 0.4 fusion.17
  95.3 0.2 fusion.18
  95.5 29.5 %psum.30 = f32[1024]{0:T(1024)S(1)} all-reduce(f32[1024]{0:T(1024)S(1)} %bitcast.30), channel_id=1, replica_groups=mesh['fish'=2,'img'=16] {'img'}, use_global_device_ids=true, to_apply=%region_4.0 | all-reduce | flops 1024 | bytes 8192 | tf_op jit(solution)/shard_map/psum | solution.py:43
  125.0 0.4 fusion.19
  125.4 1.3 fusion.4
  126.7 0.2 fusion.20
  127.0 29.5 %psum.31 = f32[1024]{0:T(1024)S(1)} all-reduce(f32[1024]{0:T(1024)S(1)} %bitcast.31), channel_id=1, replica_groups=mesh['fish'=2,'img'=16] {'img'}, use_global_device_ids=true, to_apply=%region_5.0 | all-reduce | flops 1024 | bytes 8192 | tf_op jit(solution)/shard_map/psum | solution.py:43
  156.5 0.1 dynamic_slice.3
  156.6 1.3 fusion
  157.9 22.0 %reduce-scatter.2.cloned.1.call-done = f32[64,64]{1,0:T(8,128)} async-done(((f32[1024,64]{1,0:T(8,128)}), f32[64,64]{1,0:T(8,128)}) %reduce-scatter.2.cloned.1.call-update) | async-done | bytes 16400 | tf_op jit(solution)/shard_map/reduce_scatter | solution.py:53
  180.0 0.8 negate_bitcast_fusion
  180.8 0.7 copy.8
  (25 shorter events, 0.2 us)
Async XLA Ops:
  7.2 172.8 %reduce-scatter.2.cloned.1.call-start = ((), (), s32[]{:S(2)}) async-start(), calls=%async_computation.1 | async-start | bytes 557056 | tf_op jit(solution)/shard_map/reduce_scatter | solution.py:53
  32.9 1.7 copy-start.2
  34.2 30.5 %copy-start.1 = (f32[1024]{0:T(1024)S(1)}, f32[1024]{0:T(1024)}, u32[]{:S(2)}) copy-start(f32[1024]{0:T(1024)} %param.7) | copy-start | bytes 12292
  95.3 30.1 %copy-start = (bf16[64,512]{1,0:T(8,128)(2,1)S(1)}, bf16[64,512]{1,0:T(8,128)(2,1)}, u32[]{:S(2)}) copy-start(bf16[64,512]{1,0:T(8,128)(2,1)} %param.4) | copy-start | bytes 196612
Sparse Core Ops, SparseCore 0:
  126.9 53.0 reduce-scatter.1
where the time goes:
time: 189 us; the launch traced here: 188 us
  blocking collectives  142 us (75%)
  waiting for transfers between devices  22.1 us (12%)
  between operations  14.1 us (7%)
  matrix products  6.44 us (3%)
  other arithmetic  1.98 us (1%)
    psum x4, blocking collectives, shards(): col_scale = mdl_mass / lax.psum(partial_cols, 'img')  118 us
    all_gather x1, blocking collectives, shards(): model_unit = lax.all_gather(normalize(mdl_feat), 'img', axis=1, tiled=True)  23.8 us
    reduce_scatter x1, waiting for transfers between devices, shards(): lax.psum_scatter(lax.dot_general(kernel, row_feat, (((0,), (1,)), ((), ()...  22 us
  transfers between devices with their start and end apart: 1, of which 1 were waited for; matrix products, arithmetic and copies ran while one was open for 1% of the time, Pallas kernels for 0%

commit v1 on v0

v1 whole, which is shorter than its diff:
```python
import functools

import jax
import jax.numpy as jnp
from jax import lax
from jax.experimental import pallas as pl
from jax.experimental.pallas import tpu as pltpu
from jax.sharding import PartitionSpec as P

FEAT = 64
ITERS = 4
LANES = 128
HALF = 64
REP = 16

inv_temp = 20.0


def normalize(features):
    wide = features.astype(jnp.float32)
    guarded = jnp.mean(wide * wide, axis=0, keepdims=True) + 1e-06
    return wide * lax.rsqrt(guarded)


def repeat(count, body):
    if count <= 16:
        for step in range(count):
            body(step)
    else:
        lax.fori_loop(0, count, lambda step, carry: (body(step), carry)[1], 0)


def whole_kernel(
    n, img_ref, mdl_ref, img_mass_ref, mdl_mass_ref, grad_img_ref, grad_mdl_ref,
    units, model, kern, parts, scale, feat_out, feat_in, send_sem, recv_sem,
):
    me = lax.axis_index("img")
    total = kern.shape[1]
    lines = total // LANES

    def partner(step):
        return lax.rem(me + step + 1, n)

    def send(phase, source, target_slot):
        def one(step):
            to = partner(step)
            pltpu.make_async_remote_copy(
                src_ref=source(to),
                dst_ref=target_slot,
                send_sem=send_sem.at[phase],
                recv_sem=recv_sem.at[phase],
                device_id={"img": to},
                device_id_type=pl.DeviceIdType.MESH,
            ).start()

        repeat(n - 1, one)

    def arrived(phase, slots):
        all_but_own = slots.at[pl.ds(0, n - 1)]
        pltpu.make_async_copy(all_but_own, all_but_own, recv_sem.at[phase]).wait()

    def sent(phase, slots):
        all_but_own = slots.at[pl.ds(0, n - 1)]
        pltpu.make_async_copy(all_but_own, all_but_own, send_sem.at[phase]).wait()

    barrier = pltpu.get_barrier_semaphore()

    def greet(step):
        pl.semaphore_signal(
            barrier, inc=1, device_id={"img": partner(step)}, device_id_type=pl.DeviceIdType.MESH
        )

    repeat(n - 1, greet)

    own = normalize(mdl_ref[...])
    units[me] = jnp.concatenate([own[: FEAT // 2], own[FEAT // 2 :]], axis=1).astype(jnp.bfloat16)
    pl.semaphore_wait(barrier, n - 1)
    send(0, lambda to: units.at[me], units.at[me])

    img_unit = normalize(img_ref[...]).astype(jnp.bfloat16)
    img_rows = img_unit.astype(jnp.float32).T.astype(jnp.bfloat16)
    img_mass = img_mass_ref[...]
    left = lax.broadcasted_iota(jnp.int32, (FEAT // 2, LANES), 1) < HALF

    arrived(0, units)

    factor = inv_temp / FEAT
    chunk = 2 * LANES

    def build(step):
        blocks = []
        for sub in range(chunk // LANES):
            pair = step * (chunk // LANES) + sub
            one = units[2 * pair].astype(jnp.float32)
            two = units[2 * pair + 1].astype(jnp.float32)
            top = jnp.where(left, one, pltpu.roll(two, HALF, 1))
            bottom = jnp.where(left, pltpu.roll(one, HALF, 1), two)
            blocks.append(jnp.concatenate([top, bottom], axis=0))
        columns = jnp.concatenate(blocks, axis=1).astype(jnp.bfloat16)
        where = pl.ds(step * chunk if isinstance(step, int) else pl.multiple_of(step * chunk, chunk), chunk)
        model[:, where] = columns
        scores = jnp.dot(img_rows, columns, preferred_element_type=jnp.float32)
        kern[:, where] = jnp.exp(scores * factor).astype(jnp.bfloat16)

    repeat(total // chunk, build)

    col_wide = jnp.ones((REP, total), jnp.float32)
    for iteration in range(ITERS):
        row_sums = lax.dot_general(
            col_wide.astype(jnp.bfloat16), kern[...], (((1,), (1,)), ((), ())),
            preferred_element_type=jnp.float32,
        )
        row_scale = img_mass / row_sums
        partial_cols = jnp.dot(
            row_scale.astype(jnp.bfloat16), kern[...], preferred_element_type=jnp.float32
        )
        for line in range(lines):
            parts[iteration, me, line : line + 1, :] = partial_cols[:1, line * LANES : (line + 1) * LANES]
        send(1 + iteration, lambda to: parts.at[iteration, me], parts.at[iteration, me])

        if iteration == ITERS - 1:
            row_feat = (img_unit.astype(jnp.float32) * row_scale[:1]).astype(jnp.bfloat16)
            for pair in range(n // 2):
                both = jnp.dot(
                    row_feat, kern[:, pair * LANES : (pair + 1) * LANES],
                    preferred_element_type=jnp.float32,
                )
                top, bottom = both[: FEAT // 2], both[FEAT // 2 :]
                feat_out[2 * pair] = jnp.where(left, top, pltpu.roll(bottom, HALF, 1)).astype(jnp.bfloat16)
                feat_out[2 * pair + 1] = jnp.where(left, pltpu.roll(top, HALF, 1), bottom).astype(jnp.bfloat16)
            send(1 + ITERS, lambda to: feat_out.at[to], feat_in.at[me])

        arrived(1 + iteration, parts.at[iteration])
        col_sum = jnp.sum(parts[iteration], axis=0)
        scale[...] = mdl_mass_ref[...] / col_sum
        col_wide = jnp.concatenate(
            [jnp.broadcast_to(scale[line : line + 1, :], (REP, LANES)) for line in range(lines)], axis=1
        )

    weighted = (model[...].astype(jnp.float32) * col_wide[:1]).astype(jnp.bfloat16)
    image_terms = lax.dot_general(
        weighted, kern[...], (((1,), (1,)), ((), ())), preferred_element_type=jnp.float32
    )
    grad_img_ref[...] = -(image_terms * row_scale[:1])

    feat_in[me] = feat_out[me]
    arrived(1 + ITERS, feat_in)
    summed = jnp.sum(feat_in[...].astype(jnp.float32), axis=0)
    line = scale[pl.ds(me // 2, 1), :]
    even = lax.rem(me, 2) == 0
    own_scale = jnp.where(left[:1] == even, line, pltpu.roll(line, HALF, 1))
    packed = -(summed * own_scale)
    grad_mdl_ref[: FEAT // 2] = packed[:, :HALF]
    grad_mdl_ref[FEAT // 2 :] = pltpu.roll(packed, HALF, 1)[:, :HALF]

    sent(0, units)
    for iteration in range(ITERS):
        sent(1 + iteration, parts.at[iteration])
    sent(1 + ITERS, feat_out)


def shards(n, img_feat, mdl_feat, img_mass, mdl_mass):
    rows = img_feat.shape[1]
    share = mdl_feat.shape[1]
    total = share * n
    assert share == HALF and img_feat.shape[0] == FEAT
    lines = total // LANES
    vmem = pl.BlockSpec(memory_space=pltpu.VMEM)
    packed = (n, FEAT // 2, LANES)
    return pl.pallas_call(
        functools.partial(whole_kernel, n),
        out_shape=(
            jax.ShapeDtypeStruct((FEAT, rows), jnp.float32),
            jax.ShapeDtypeStruct((FEAT, share), jnp.float32),
        ),
        in_specs=[vmem] * 4,
        out_specs=(vmem, vmem),
        scratch_shapes=[
            pltpu.VMEM(packed, jnp.bfloat16),
            pltpu.VMEM((FEAT, total), jnp.bfloat16),
            pltpu.VMEM((rows, total), jnp.bfloat16),
            pltpu.VMEM((ITERS, n, lines, LANES), jnp.float32),
            pltpu.VMEM((lines, LANES), jnp.float32),
            pltpu.VMEM(packed, jnp.bfloat16),
            pltpu.VMEM(packed, jnp.bfloat16),
            pltpu.SemaphoreType.DMA((2 + ITERS,)),
            pltpu.SemaphoreType.DMA((2 + ITERS,)),
        ],
        compiler_params=pltpu.CompilerParams(
            collective_id=0, has_side_effects=True, vmem_limit_bytes=56 * 2**20
        ),
        name="sinkhorn",
    )(img_feat, mdl_feat, img_mass.reshape(1, rows), mdl_mass.reshape(lines, LANES))


def solution(mesh):
    placed = (P(None, ("fish", "img")), P(None, ("fish", "img")), P(("fish", "img")), P("fish"))
    return jax.shard_map(
        functools.partial(shards, mesh.shape["img"]),
        mesh=mesh,
        in_specs=placed,
        out_specs=(P(None, ("fish", "img")), P(None, ("fish", "img"))),
        check_vma=False,
    )
```

time: 189 us -> 36.7 us (0.19)
  blocking collectives: 142 us -> 0 us
  Pallas kernels: 0 us -> 33.7 us
  waiting for transfers between devices: 22.1 us -> 0 us
  between operations: 14.1 us -> 0.65 us
  matrix products: 6.44 us -> 0 us
  other arithmetic: 1.98 us -> 0 us
    psum x4 -> x0, blocking collectives: 118 us -> none  [shards(): col_scale = mdl_mass / lax.psum(partial_cols, 'img')]
    pallas_call x0 -> x1, Pallas kernels: none -> 33.7 us  [shards(): pl.pallas_call(functools.partial(whole_kernel, n), out_shape=(jax.ShapeDt...]
    all_gather x1 -> x0, blocking collectives: 23.8 us -> none  [shards(): model_unit = lax.all_gather(normalize(mdl_feat), 'img', axis=1, tiled=True)]
    reduce_scatter x1 -> x0, waiting for transfers between devices: 22 us -> none  [shards(): lax.psum_scatter(lax.dot_general(kernel, row_feat, (((0,), (1,)), ((), ()...]
    dot_general x11 -> x0, matrix products: 6.44 us -> none  [the longest x4 1.49 us: shards(): jnp.dot(kernel, col_low, preferred_element_type=jnp.float32)]
  transfers between devices with their start and end apart: 1 -> 0, of which waited for: 1 -> 0; matrix products, arithmetic and copies ran while one was open for 1% -> 0% of each run, Pallas kernels for 0% -> 0%
where the time goes in v1:
time: 36.7 us; the launch traced here: 36.5 us
  Pallas kernels  33.7 us (92%)
  local copies, waits for them, and re-layouts  2.19 us (6%)
  between operations  0.65 us (2%)
    pallas_call x1, Pallas kernels, shards(): pl.pallas_call(functools.partial(whole_kernel, n), out_shape=(jax.ShapeDt...  33.7 us
    unnamed x4, local copies, waits for them, and re-layouts  2.19 us

profile of v1, /device:TPU:0, one launch (start us, length us, event | category | flops | bytes accessed | tf_op | source)
XLA Modules:
  0.0 36.5 jit_solution(15085670995118100337)
XLA Ops:
  0.6 33.7 %sinkhorn.1 = (f32[64,512]{1,0:T(8,128)}, f32[64,64]{1,0:T(8,128)}) custom-call(bf16[64,512]{1,0:T(8,128)(2,1)} %img_ref.1, bf16[64,64]{1,0:T(8,128)(2,1)} %mdl_ref.1, f32[1,512]{1,0:T(1,128)} %bitcast.3, f32[8,128]{1,0:T(8,128)} %bitcast.2), custom_call_target="tpu_custom_call" | custom-call | tf_op jit(solution)/shard_map/sinkhorn/pallas_call | solution.py:170
  34.3 0.0 copy-start
  34.3 1.6 %copy.8 = f32[64,512]{1,0:T(8,128)} copy(f32[64,512]{1,0:T(8,128)} %get-tuple-element.4) | data formatting | bytes 262144
  35.9 0.0 copy-done
  35.9 0.6 %copy.9 = f32[64,64]{1,0:T(8,128)} copy(f32[64,64]{1,0:T(8,128)S(1)} %copy-done) | data formatting | bytes 32768
Async XLA Ops:
  34.3 1.6 %copy-start = (f32[64,64]{1,0:T(8,128)S(1)}, f32[64,64]{1,0:T(8,128)}, u32[]{:S(2)}) copy-start(f32[64,64]{1,0:T(8,128)} %get-tuple-element.5) | copy-start | bytes 49156

commit v2 on v1

--- a/solution.py
+++ b/solution.py
@@ -31,8 +31,9 @@
 
 
 def whole_kernel(
-    n, img_ref, mdl_ref, img_mass_ref, mdl_mass_ref, grad_img_ref, grad_mdl_ref,
-    units, model, kern, parts, scale, feat_out, feat_in, send_sem, recv_sem,
+    n, img_hbm, mdl_hbm, img_mass_hbm, mdl_mass_hbm, grad_img_ref, grad_mdl_ref,
+    img_ref, mdl_ref, img_mass_ref, mdl_mass_ref,
+    units, model, kern, parts, scale, feat_out, feat_in, load_sem, send_sem, recv_sem,
 ):
     me = lax.axis_index("img")
     total = kern.shape[1]
@@ -70,13 +71,24 @@
             barrier, inc=1, device_id={"img": partner(step)}, device_id_type=pl.DeviceIdType.MESH
         )
 
+    loads = [
+        pltpu.make_async_copy(source, target, load_sem.at[slot])
+        for slot, (source, target) in enumerate(
+            ((mdl_hbm, mdl_ref), (img_hbm, img_ref), (img_mass_hbm, img_mass_ref), (mdl_mass_hbm, mdl_mass_ref))
+        )
+    ]
+    for load in loads:
+        load.start()
     repeat(n - 1, greet)
+    loads[0].wait()
 
     own = normalize(mdl_ref[...])
     units[me] = jnp.concatenate([own[: FEAT // 2], own[FEAT // 2 :]], axis=1).astype(jnp.bfloat16)
     pl.semaphore_wait(barrier, n - 1)
     send(0, lambda to: units.at[me], units.at[me])
 
+    for load in loads[1:]:
+        load.wait()
     img_unit = normalize(img_ref[...]).astype(jnp.bfloat16)
     img_rows = img_unit.astype(jnp.float32).T.astype(jnp.bfloat16)
     img_mass = img_mass_ref[...]
@@ -159,6 +171,17 @@
     sent(1 + ITERS, feat_out)
 
 
+def store_kernel(grad_img_ref, grad_mdl_ref, grad_img_hbm, grad_mdl_hbm, sems):
+    stores = [
+        pltpu.make_async_copy(grad_img_ref, grad_img_hbm, sems.at[0]),
+        pltpu.make_async_copy(grad_mdl_ref, grad_mdl_hbm, sems.at[1]),
+    ]
+    for store in stores:
+        store.start()
+    for store in stores:
+        store.wait()
+
+
 def shards(n, img_feat, mdl_feat, img_mass, mdl_mass):
     rows = img_feat.shape[1]
     share = mdl_feat.shape[1]
@@ -167,15 +190,20 @@
     lines = total // LANES
     vmem = pl.BlockSpec(memory_space=pltpu.VMEM)
     packed = (n, FEAT // 2, LANES)
-    return pl.pallas_call(
+    anywhere = pl.BlockSpec(memory_space=pl.ANY)
+    grads = pl.pallas_call(
         functools.partial(whole_kernel, n),
         out_shape=(
-            jax.ShapeDtypeStruct((FEAT, rows), jnp.float32),
-            jax.ShapeDtypeStruct((FEAT, share), jnp.float32),
+            pltpu.VMEM((FEAT, rows), jnp.float32),
+            pltpu.VMEM((FEAT, share), jnp.float32),
         ),
-        in_specs=[vmem] * 4,
+        in_specs=[pl.BlockSpec(memory_space=pltpu.HBM)] * 4,
         out_specs=(vmem, vmem),
         scratch_shapes=[
+            pltpu.VMEM((FEAT, rows), jnp.bfloat16),
+            pltpu.VMEM((FEAT, share), jnp.bfloat16),
+            pltpu.VMEM((1, rows), jnp.float32),
+            pltpu.VMEM((lines, LANES), jnp.float32),
             pltpu.VMEM(packed, jnp.bfloat16),
             pltpu.VMEM((FEAT, total), jnp.bfloat16),
             pltpu.VMEM((rows, total), jnp.bfloat16),
@@ -183,14 +211,26 @@
             pltpu.VMEM((lines, LANES), jnp.float32),
             pltpu.VMEM(packed, jnp.bfloat16),
             pltpu.VMEM(packed, jnp.bfloat16),
+            pltpu.SemaphoreType.DMA((4,)),
             pltpu.SemaphoreType.DMA((2 + ITERS,)),
             pltpu.SemaphoreType.DMA((2 + ITERS,)),
         ],
         compiler_params=pltpu.CompilerParams(
-            collective_id=0, has_side_effects=True, vmem_limit_bytes=56 * 2**20
+            collective_id=0, has_side_effects=True, vmem_limit_bytes=60 * 2**20
         ),
         name="sinkhorn",
     )(img_feat, mdl_feat, img_mass.reshape(1, rows), mdl_mass.reshape(lines, LANES))
+    return pl.pallas_call(
+        store_kernel,
+        out_shape=(
+            jax.ShapeDtypeStruct((FEAT, rows), jnp.float32),
+            jax.ShapeDtypeStruct((FEAT, share), jnp.float32),
+        ),
+        in_specs=[vmem] * 2,
+        out_specs=(anywhere, anywhere),
+        scratch_shapes=[pltpu.SemaphoreType.DMA((2,))],
+        name="store",
+    )(*grads)
 
 
 def solution(mesh):

time: 36.7 us -> 36 us (0.981)
  local copies, waits for them, and re-layouts: 2.19 us -> 1.25 us
    unnamed x4, local copies, waits for them, and re-layouts: 2.19 us -> 1.25 us
    pallas_call x1 -> x2, Pallas kernels: 33.7 us -> 33.8 us  [the longest x1 32.2 us: shards(): pl.pallas_call(functools.partial(whole_kernel, n), out_shape=(pltpu.VMEM(...]
where the time goes in v2:
time: 36 us; the launch traced here: 35.7 us
  Pallas kernels  33.8 us (94%)
  local copies, waits for them, and re-layouts  1.25 us (3%)
  between operations  0.65 us (2%)
    pallas_call x1, Pallas kernels, shards(): pl.pallas_call(functools.partial(whole_kernel, n), out_shape=(pltpu.VMEM(...  32.2 us
    pallas_call x1, Pallas kernels, shards(): pl.pallas_call(store_kernel, out_shape=(jax.ShapeDtypeStruct((FEAT, rows)...  1.58 us
    unnamed x4, local copies, waits for them, and re-layouts  1.25 us

profile of v2, /device:TPU:0, one launch (start us, length us, event | category | flops | bytes accessed | tf_op | source)
XLA Modules:
  0.0 35.7 jit_solution(5807938234044897126)
XLA Ops:
  0.6 32.2 %sinkhorn.1 = (f32[64,512]{1,0:T(8,128)S(1)}, f32[64,64]{1,0:T(8,128)S(1)}) custom-call(bf16[64,512]{1,0:T(8,128)(2,1)} %img_hbm.1, bf16[64,64]{1,0:T(8,128)(2,1)} %mdl_hbm.1, f32[1,512]{1,0:T(1,128)} %bitcast.3, f32[8,128]{1,0:T(8,128)} %bitcast.2), custom_call_target="tpu_custom_call" | custom-call | tf_op jit(solution)/shard_map/sinkhorn/pallas_call | solution.py:194
  32.9 0.0 copy-start
  32.9 0.6 %copy-done = f32[64,512]{1,0:T(8,128)} copy-done((f32[64,512]{1,0:T(8,128)}, f32[64,512]{1,0:T(8,128)S(1)}, u32[]{:S(2)}) %copy-start) | copy-done | bytes 131096
  33.5 0.0 copy-start.1
  33.5 0.6 %copy-done.1 = f32[64,64]{1,0:T(8,128)} copy-done((f32[64,64]{1,0:T(8,128)}, f32[64,64]{1,0:T(8,128)S(1)}, u32[]{:S(2)}) %copy-start.1) | copy-done | bytes 16408
  34.1 1.6 %store.1 = (f32[64,512]{1,0:T(8,128)}, f32[64,64]{1,0:T(8,128)}) custom-call(f32[64,512]{1,0:T(8,128)} %copy-done, f32[64,64]{1,0:T(8,128)} %copy-done.1), custom_call_target="tpu_custom_call" | custom-call | tf_op jit(solution)/shard_map/store/pallas_call | solution.py:223
Async XLA Ops:
  32.9 0.6 %copy-start = (f32[64,512]{1,0:T(8,128)}, f32[64,512]{1,0:T(8,128)S(1)}, u32[]{:S(2)}) copy-start(f32[64,512]{1,0:T(8,128)S(1)} %get-tuple-element.4.grad_img_ref) | copy-start | bytes 393220
  33.5 0.6 %copy-start.1 = (f32[64,64]{1,0:T(8,128)}, f32[64,64]{1,0:T(8,128)S(1)}, u32[]{:S(2)}) copy-start(f32[64,64]{1,0:T(8,128)S(1)} %get-tuple-element.5.grad_mdl_ref) | copy-start | bytes 49156

commit v3 on v2

--- a/solution.py
+++ b/solution.py
@@ -30,21 +30,38 @@
         lax.fori_loop(0, count, lambda step, carry: (body(step), carry)[1], 0)
 
 
+def near_group(n):
+    size = 1
+    while (2 * size) ** 2 <= n and n % (2 * size) == 0:
+        size *= 2
+    return size
+
+
 def whole_kernel(
     n, img_hbm, mdl_hbm, img_mass_hbm, mdl_mass_hbm, grad_img_ref, grad_mdl_ref,
     img_ref, mdl_ref, img_mass_ref, mdl_mass_ref,
-    units, model, kern, parts, scale, feat_out, feat_in, load_sem, send_sem, recv_sem,
+    units, model, kern, parts, sums, scale, feat_out, feat_in, load_sem, send_sem, recv_sem,
 ):
     me = lax.axis_index("img")
     total = kern.shape[1]
     lines = total // LANES
 
+    inner = near_group(n)
+    outer = n // inner
+    my_inner, my_outer = lax.rem(me, inner), me // inner
+
     def partner(step):
         return lax.rem(me + step + 1, n)
 
-    def send(phase, source, target_slot):
+    def near(step):
+        return my_outer * inner + lax.rem(my_inner + step + 1, inner)
+
+    def far(step):
+        return lax.rem(my_outer + step + 1, outer) * inner + my_inner
+
+    def send(phase, count, whom, source, target_slot):
         def one(step):
-            to = partner(step)
+            to = whom(step)
             pltpu.make_async_remote_copy(
                 src_ref=source(to),
                 dst_ref=target_slot,
@@ -54,14 +71,14 @@
                 device_id_type=pl.DeviceIdType.MESH,
             ).start()
 
-        repeat(n - 1, one)
-
-    def arrived(phase, slots):
-        all_but_own = slots.at[pl.ds(0, n - 1)]
+        repeat(count - 1, one)
+
+    def arrived(phase, count, slots):
+        all_but_own = slots.at[pl.ds(0, count - 1)]
         pltpu.make_async_copy(all_but_own, all_but_own, recv_sem.at[phase]).wait()
 
-    def sent(phase, slots):
-        all_but_own = slots.at[pl.ds(0, n - 1)]
+    def sent(phase, count, slots):
+        all_but_own = slots.at[pl.ds(0, count - 1)]
         pltpu.make_async_copy(all_but_own, all_but_own, send_sem.at[phase]).wait()
 
     barrier = pltpu.get_barrier_semaphore()
@@ -85,7 +102,7 @@
     own = normalize(mdl_ref[...])
     units[me] = jnp.concatenate([own[: FEAT // 2], own[FEAT // 2 :]], axis=1).astype(jnp.bfloat16)
     pl.semaphore_wait(barrier, n - 1)
-    send(0, lambda to: units.at[me], units.at[me])
+    send(0, n, partner, lambda to: units.at[me], units.at[me])
 
     for load in loads[1:]:
         load.wait()
@@ -94,7 +111,7 @@
     img_mass = img_mass_ref[...]
     left = lax.broadcasted_iota(jnp.int32, (FEAT // 2, LANES), 1) < HALF
 
-    arrived(0, units)
+    arrived(0, n, units)
 
     factor = inv_temp / FEAT
     chunk = 2 * LANES
@@ -127,8 +144,10 @@
             row_scale.astype(jnp.bfloat16), kern[...], preferred_element_type=jnp.float32
         )
         for line in range(lines):
-            parts[iteration, me, line : line + 1, :] = partial_cols[:1, line * LANES : (line + 1) * LANES]
-        send(1 + iteration, lambda to: parts.at[iteration, me], parts.at[iteration, me])
+            parts[iteration, my_inner, line : line + 1, :] = partial_cols[:1, line * LANES : (line + 1) * LANES]
+        first = 2 + 2 * iteration
+        mine = parts.at[iteration, my_inner]
+        send(first, inner, near, lambda to: mine, mine)
 
         if iteration == ITERS - 1:
             row_feat = (img_unit.astype(jnp.float32) * row_scale[:1]).astype(jnp.bfloat16)
@@ -140,10 +159,14 @@
                 top, bottom = both[: FEAT // 2], both[FEAT // 2 :]
                 feat_out[2 * pair] = jnp.where(left, top, pltpu.roll(bottom, HALF, 1)).astype(jnp.bfloat16)
                 feat_out[2 * pair + 1] = jnp.where(left, pltpu.roll(top, HALF, 1), bottom).astype(jnp.bfloat16)
-            send(1 + ITERS, lambda to: feat_out.at[to], feat_in.at[me])
-
-        arrived(1 + iteration, parts.at[iteration])
-        col_sum = jnp.sum(parts[iteration], axis=0)
+            send(1, n, partner, lambda to: feat_out.at[to], feat_in.at[me])
+
+        arrived(first, inner, parts.at[iteration])
+        sums[iteration, my_outer] = jnp.sum(parts[iteration], axis=0)
+        group = sums.at[iteration, my_outer]
+        send(first + 1, outer, far, lambda to: group, group)
+        arrived(first + 1, outer, sums.at[iteration])
+        col_sum = jnp.sum(sums[iteration], axis=0)
         scale[...] = mdl_mass_ref[...] / col_sum
         col_wide = jnp.concatenate(
             [jnp.broadcast_to(scale[line : line + 1, :], (REP, LANES)) for line in range(lines)], axis=1
@@ -156,7 +179,7 @@
     grad_img_ref[...] = -(image_terms * row_scale[:1])
 
     feat_in[me] = feat_out[me]
-    arrived(1 + ITERS, feat_in)
+    arrived(1, n, feat_in)
     summed = jnp.sum(feat_in[...].astype(jnp.float32), axis=0)
     line = scale[pl.ds(me // 2, 1), :]
     even = lax.rem(me, 2) == 0
@@ -165,10 +188,11 @@
     grad_mdl_ref[: FEAT // 2] = packed[:, :HALF]
     grad_mdl_ref[FEAT // 2 :] = pltpu.roll(packed, HALF, 1)[:, :HALF]
 
-    sent(0, units)
+    sent(0, n, units)
+    sent(1, n, feat_out)
     for iteration in range(ITERS):
-        sent(1 + iteration, parts.at[iteration])
-    sent(1 + ITERS, feat_out)
+        sent(2 + 2 * iteration, inner, parts.at[iteration])
+        sent(3 + 2 * iteration, outer, sums.at[iteration])
 
 
 def store_kernel(grad_img_ref, grad_mdl_ref, grad_img_hbm, grad_mdl_hbm, sems):
@@ -207,13 +231,14 @@
             pltpu.VMEM(packed, jnp.bfloat16),
             pltpu.VMEM((FEAT, total), jnp.bfloat16),
             pltpu.VMEM((rows, total), jnp.bfloat16),
-            pltpu.VMEM((ITERS, n, lines, LANES), jnp.float32),
+            pltpu.VMEM((ITERS, near_group(n), lines, LANES), jnp.float32),
+            pltpu.VMEM((ITERS, n // near_group(n), lines, LANES), jnp.float32),
             pltpu.VMEM((lines, LANES), jnp.float32),
             pltpu.VMEM(packed, jnp.bfloat16),
             pltpu.VMEM(packed, jnp.bfloat16),
             pltpu.SemaphoreType.DMA((4,)),
-            pltpu.SemaphoreType.DMA((2 + ITERS,)),
-            pltpu.SemaphoreType.DMA((2 + ITERS,)),
+            pltpu.SemaphoreType.DMA((2 + 2 * ITERS,)),
+            pltpu.SemaphoreType.DMA((2 + 2 * ITERS,)),
         ],
         compiler_params=pltpu.CompilerParams(
             collective_id=0, has_side_effects=True, vmem_limit_bytes=60 * 2**20
@@ -229,6 +254,7 @@
         in_specs=[vmem] * 2,
         out_specs=(anywhere, anywhere),
         scratch_shapes=[pltpu.SemaphoreType.DMA((2,))],
+        compiler_params=pltpu.CompilerParams(vmem_limit_bytes=2**20),
         name="store",
     )(*grads)
 

time: 36 us -> 39.3 us (1.092)
  Pallas kernels: 33.8 us -> 38.4 us
  local copies, waits for them, and re-layouts: 1.25 us -> 0 us
    pallas_call x1, Pallas kernels: 32.2 us -> 37.8 us  [shards(): pl.pallas_call(functools.partial(whole_kernel, n), out_shape=(pltpu.VMEM(...]
    unnamed x4 -> x0, local copies, waits for them, and re-layouts: 1.25 us -> none
    pallas_call x1, Pallas kernels: 1.58 us -> 0.68 us  [shards(): pl.pallas_call(store_kernel, out_shape=(jax.ShapeDtypeStruct((FEAT, rows)...]
where the time goes in v3:
time: 39.3 us; the launch traced here: 39.1 us
  Pallas kernels  38.4 us (98%)
  between operations  0.64 us (2%)
    pallas_call x1, Pallas kernels, shards(): pl.pallas_call(functools.partial(whole_kernel, n), out_shape=(pltpu.VMEM(...  37.8 us

profile of v3, /device:TPU:0, one launch (start us, length us, event | category | flops | bytes accessed | tf_op | source)
XLA Modules:
  0.0 39.1 jit_solution(3567612310135588471)
XLA Ops:
  0.6 37.8 %sinkhorn.1 = (f32[64,512]{1,0:T(8,128)S(1)}, f32[64,64]{1,0:T(8,128)S(1)}) custom-call(bf16[64,512]{1,0:T(8,128)(2,1)} %img_hbm.1, bf16[64,64]{1,0:T(8,128)(2,1)} %mdl_hbm.1, f32[1,512]{1,0:T(1,128)} %bitcast.3, f32[8,128]{1,0:T(8,128)} %bitcast.2), custom_call_target="tpu_custom_call" | custom-call | tf_op jit(solution)/shard_map/sinkhorn/pallas_call | solution.py:218
  38.4 0.7 %store.1 = (f32[64,512]{1,0:T(8,128)}, f32[64,64]{1,0:T(8,128)}) custom-call(f32[64,512]{1,0:T(8,128)S(1)} %get-tuple-element.4.grad_img_ref, f32[64,64]{1,0:T(8,128)S(1)} %get-tuple-element.5.grad_mdl_ref), custom_call_target="tpu_custom_call" | custom-call | tf_op jit(solution)/shard_map/store/pallas_call | solution.py:248

commit v4 on v2

--- a/solution.py
+++ b/solution.py
@@ -22,37 +22,49 @@
     return wide * lax.rsqrt(guarded)
 
 
-def repeat(count, body):
+def repeat(count, body, carry=0):
     if count <= 16:
         for step in range(count):
-            body(step)
-    else:
-        lax.fori_loop(0, count, lambda step, carry: (body(step), carry)[1], 0)
+            carry = body(step, carry)
+        return carry
+    return lax.fori_loop(0, count, body, carry)
+
+
+def other(index, step, count):
+    if not isinstance(step, int) or count & (count - 1):
+        return lax.rem(index + step, count)
+    bit = 1
+    while bit <= step:
+        if step & bit:
+            index = index + bit * (1 - 2 * lax.rem(index // bit, 2))
+        bit *= 2
+    return index
 
 
 def whole_kernel(
     n, img_hbm, mdl_hbm, img_mass_hbm, mdl_mass_hbm, grad_img_ref, grad_mdl_ref,
     img_ref, mdl_ref, img_mass_ref, mdl_mass_ref,
-    units, model, kern, parts, scale, feat_out, feat_in, load_sem, send_sem, recv_sem,
+    units, model, kern, parts, scale, feat_out, feat_in, load_sem, unit_sem, send_sem, recv_sem,
 ):
     me = lax.axis_index("img")
     total = kern.shape[1]
     lines = total // LANES
 
     def partner(step):
-        return lax.rem(me + step + 1, n)
-
-    def send(phase, source, target_slot):
-        def one(step):
+        return other(me, n - 1 - step, n)
+
+    def send(phase, source, target_slot, landed):
+        def one(step, carry):
             to = partner(step)
             pltpu.make_async_remote_copy(
                 src_ref=source(to),
                 dst_ref=target_slot,
                 send_sem=send_sem.at[phase],
-                recv_sem=recv_sem.at[phase],
+                recv_sem=landed,
                 device_id={"img": to},
                 device_id_type=pl.DeviceIdType.MESH,
             ).start()
+            return carry
 
         repeat(n - 1, one)
 
@@ -66,10 +78,11 @@
 
     barrier = pltpu.get_barrier_semaphore()
 
-    def greet(step):
+    def greet(step, carry):
         pl.semaphore_signal(
             barrier, inc=1, device_id={"img": partner(step)}, device_id_type=pl.DeviceIdType.MESH
         )
+        return carry
 
     loads = [
         pltpu.make_async_copy(source, target, load_sem.at[slot])
@@ -85,7 +98,7 @@
     own = normalize(mdl_ref[...])
     units[me] = jnp.concatenate([own[: FEAT // 2], own[FEAT // 2 :]], axis=1).astype(jnp.bfloat16)
     pl.semaphore_wait(barrier, n - 1)
-    send(0, lambda to: units.at[me], units.at[me])
+    send(0, lambda to: units.at[me], units.at[me], unit_sem.at[me])
 
     for load in loads[1:]:
         load.wait()
@@ -94,41 +107,52 @@
     img_mass = img_mass_ref[...]
     left = lax.broadcasted_iota(jnp.int32, (FEAT // 2, LANES), 1) < HALF
 
-    arrived(0, units)
-
     factor = inv_temp / FEAT
     chunk = 2 * LANES
-
-    def build(step):
+    group = chunk // HALF
+    ones = jnp.ones((REP, chunk), jnp.bfloat16)
+
+    def build(step, row_sums):
+        which = other(me // group, step, n // group)
+        for sub in range(group):
+            sender = which * group + sub
+
+            @pl.when(sender != me)
+            def _():
+                pltpu.make_async_copy(units.at[sender], units.at[sender], unit_sem.at[sender]).wait()
+
         blocks = []
-        for sub in range(chunk // LANES):
-            pair = step * (chunk // LANES) + sub
-            one = units[2 * pair].astype(jnp.float32)
-            two = units[2 * pair + 1].astype(jnp.float32)
+        for sub in range(0, group, 2):
+            one = units[which * group + sub].astype(jnp.float32)
+            two = units[which * group + sub + 1].astype(jnp.float32)
             top = jnp.where(left, one, pltpu.roll(two, HALF, 1))
             bottom = jnp.where(left, pltpu.roll(one, HALF, 1), two)
             blocks.append(jnp.concatenate([top, bottom], axis=0))
         columns = jnp.concatenate(blocks, axis=1).astype(jnp.bfloat16)
-        where = pl.ds(step * chunk if isinstance(step, int) else pl.multiple_of(step * chunk, chunk), chunk)
+        where = pl.ds(pl.multiple_of(which * chunk, chunk), chunk)
         model[:, where] = columns
         scores = jnp.dot(img_rows, columns, preferred_element_type=jnp.float32)
-        kern[:, where] = jnp.exp(scores * factor).astype(jnp.bfloat16)
-
-    repeat(total // chunk, build)
-
-    col_wide = jnp.ones((REP, total), jnp.float32)
+        tile = jnp.exp(scores * factor).astype(jnp.bfloat16)
+        kern[:, where] = tile
+        return row_sums + lax.dot_general(
+            ones, tile, (((1,), (1,)), ((), ())), preferred_element_type=jnp.float32
+        )
+
+    row_sums = repeat(total // chunk, build, jnp.zeros((REP, kern.shape[0]), jnp.float32))
+
     for iteration in range(ITERS):
-        row_sums = lax.dot_general(
-            col_wide.astype(jnp.bfloat16), kern[...], (((1,), (1,)), ((), ())),
-            preferred_element_type=jnp.float32,
-        )
+        if iteration > 0:
+            row_sums = lax.dot_general(
+                col_wide.astype(jnp.bfloat16), kern[...], (((1,), (1,)), ((), ())),
+                preferred_element_type=jnp.float32,
+            )
         row_scale = img_mass / row_sums
         partial_cols = jnp.dot(
             row_scale.astype(jnp.bfloat16), kern[...], preferred_element_type=jnp.float32
         )
         for line in range(lines):
             parts[iteration, me, line : line + 1, :] = partial_cols[:1, line * LANES : (line + 1) * LANES]
-        send(1 + iteration, lambda to: parts.at[iteration, me], parts.at[iteration, me])
+        send(1 + iteration, lambda to: parts.at[iteration, me], parts.at[iteration, me], recv_sem.at[1 + iteration])
 
         if iteration == ITERS - 1:
             row_feat = (img_unit.astype(jnp.float32) * row_scale[:1]).astype(jnp.bfloat16)
@@ -140,7 +164,7 @@
                 top, bottom = both[: FEAT // 2], both[FEAT // 2 :]
                 feat_out[2 * pair] = jnp.where(left, top, pltpu.roll(bottom, HALF, 1)).astype(jnp.bfloat16)
                 feat_out[2 * pair + 1] = jnp.where(left, pltpu.roll(top, HALF, 1), bottom).astype(jnp.bfloat16)
-            send(1 + ITERS, lambda to: feat_out.at[to], feat_in.at[me])
+            send(1 + ITERS, lambda to: feat_out.at[to], feat_in.at[me], recv_sem.at[1 + ITERS])
 
         arrived(1 + iteration, parts.at[iteration])
         col_sum = jnp.sum(parts[iteration], axis=0)
@@ -212,6 +236,7 @@
             pltpu.VMEM(packed, jnp.bfloat16),
             pltpu.VMEM(packed, jnp.bfloat16),
             pltpu.SemaphoreType.DMA((4,)),
+            pltpu.SemaphoreType.DMA((n,)),
             pltpu.SemaphoreType.DMA((2 + ITERS,)),
             pltpu.SemaphoreType.DMA((2 + ITERS,)),
         ],
@@ -229,6 +254,7 @@
         in_specs=[vmem] * 2,
         out_specs=(anywhere, anywhere),
         scratch_shapes=[pltpu.SemaphoreType.DMA((2,))],
+        compiler_params=pltpu.CompilerParams(vmem_limit_bytes=2**20),
         name="store",
     )(*grads)
 

time: 36 us -> 34.1 us (0.947)
  local copies, waits for them, and re-layouts: 1.25 us -> 0 us
  Pallas kernels: 33.8 us -> 33.2 us
    unnamed x4 -> x0, local copies, waits for them, and re-layouts: 1.25 us -> none
    pallas_call x1, Pallas kernels: 1.58 us -> 0.68 us  [shards(): pl.pallas_call(store_kernel, out_shape=(jax.ShapeDtypeStruct((FEAT, rows)...]
where the time goes in v4:
time: 34.1 us; the launch traced here: 33.8 us
  Pallas kernels  33.2 us (97%)
  between operations  0.64 us (2%)
    pallas_call x1, Pallas kernels, shards(): pl.pallas_call(functools.partial(whole_kernel, n), out_shape=(pltpu.VMEM(...  32.5 us

profile of v4, /device:TPU:0, one launch (start us, length us, event | category | flops | bytes accessed | tf_op | source)
XLA Modules:
  0.0 33.8 jit_solution(2259082292952559086)
XLA Ops:
  0.6 32.5 %sinkhorn.1 = (f32[64,512]{1,0:T(8,128)S(1)}, f32[64,64]{1,0:T(8,128)S(1)}) custom-call(bf16[64,512]{1,0:T(8,128)(2,1)} %img_hbm.1, bf16[64,64]{1,0:T(8,128)(2,1)} %mdl_hbm.1, f32[1,512]{1,0:T(1,128)} %bitcast.3, f32[8,128]{1,0:T(8,128)} %bitcast.2), custom_call_target="tpu_custom_call" | custom-call | tf_op jit(solution)/shard_map/sinkhorn/pallas_call | solution.py:218
  33.1 0.7 %store.1 = (f32[64,512]{1,0:T(8,128)}, f32[64,64]{1,0:T(8,128)}) custom-call(f32[64,512]{1,0:T(8,128)S(1)} %get-tuple-element.4.grad_img_ref, f32[64,64]{1,0:T(8,128)S(1)} %get-tuple-element.5.grad_mdl_ref), custom_call_target="tpu_custom_call" | custom-call | tf_op jit(solution)/shard_map/store/pallas_call | solution.py:248

commit v5 on v4

--- a/solution.py
+++ b/solution.py
@@ -11,7 +11,6 @@
 ITERS = 4
 LANES = 128
 HALF = 64
-REP = 16
 
 inv_temp = 20.0
 
@@ -44,7 +43,7 @@
 def whole_kernel(
     n, img_hbm, mdl_hbm, img_mass_hbm, mdl_mass_hbm, grad_img_ref, grad_mdl_ref,
     img_ref, mdl_ref, img_mass_ref, mdl_mass_ref,
-    units, model, kern, parts, scale, feat_out, feat_in, load_sem, unit_sem, send_sem, recv_sem,
+    units, model, kern, wide, row_scale, parts, scale, feat_out, feat_in, load_sem, unit_sem, send_sem, recv_sem,
 ):
     me = lax.axis_index("img")
     total = kern.shape[1]
@@ -104,13 +103,14 @@
         load.wait()
     img_unit = normalize(img_ref[...]).astype(jnp.bfloat16)
     img_rows = img_unit.astype(jnp.float32).T.astype(jnp.bfloat16)
-    img_mass = img_mass_ref[...]
+    img_mass = jnp.broadcast_to(img_mass_ref[...], (LANES, img_rows.shape[0])).T
     left = lax.broadcasted_iota(jnp.int32, (FEAT // 2, LANES), 1) < HALF
 
     factor = inv_temp / FEAT
     chunk = 2 * LANES
     group = chunk // HALF
-    ones = jnp.ones((REP, chunk), jnp.bfloat16)
+    rows = kern.shape[0]
+    block = 64
 
     def build(step, row_sums):
         which = other(me // group, step, n // group)
@@ -134,28 +134,37 @@
         scores = jnp.dot(img_rows, columns, preferred_element_type=jnp.float32)
         tile = jnp.exp(scores * factor).astype(jnp.bfloat16)
         kern[:, where] = tile
-        return row_sums + lax.dot_general(
-            ones, tile, (((1,), (1,)), ((), ())), preferred_element_type=jnp.float32
-        )
-
-    row_sums = repeat(total // chunk, build, jnp.zeros((REP, kern.shape[0]), jnp.float32))
+        tile = tile.astype(jnp.float32)
+        wide[:, where] = tile
+        for line in range(chunk // LANES):
+            row_sums += tile[:, line * LANES : (line + 1) * LANES]
+        return row_sums
+
+    row_sums = repeat(total // chunk, build, jnp.zeros((rows, LANES), jnp.float32))
 
     for iteration in range(ITERS):
-        if iteration > 0:
-            row_sums = lax.dot_general(
-                col_wide.astype(jnp.bfloat16), kern[...], (((1,), (1,)), ((), ())),
-                preferred_element_type=jnp.float32,
-            )
-        row_scale = img_mass / row_sums
-        partial_cols = jnp.dot(
-            row_scale.astype(jnp.bfloat16), kern[...], preferred_element_type=jnp.float32
-        )
+        for start in range(0, rows, block):
+            here = slice(start, start + block)
+            if iteration == 0:
+                by_lane = row_sums[here]
+            else:
+                by_lane = jnp.zeros((block, LANES), jnp.float32)
+                for line in range(lines):
+                    by_lane += wide[here, line * LANES : (line + 1) * LANES] * col_low[line : line + 1]
+            row_scale[here] = img_mass[here] / jnp.sum(by_lane, axis=1, keepdims=True)
+        partial_cols = jnp.zeros((8, total), jnp.float32)
+        for start in range(0, rows, block):
+            here = slice(start, start + block)
+            row_low = row_scale[here, :1].astype(jnp.bfloat16).astype(jnp.float32)
+            partial_cols += jnp.sum((wide[here] * row_low).reshape(block // 8, 8, total), axis=0)
+        partial_cols = jnp.sum(partial_cols, axis=0, keepdims=True)
         for line in range(lines):
-            parts[iteration, me, line : line + 1, :] = partial_cols[:1, line * LANES : (line + 1) * LANES]
+            parts[iteration, me, line : line + 1, :] = partial_cols[:, line * LANES : (line + 1) * LANES]
         send(1 + iteration, lambda to: parts.at[iteration, me], parts.at[iteration, me], recv_sem.at[1 + iteration])
 
         if iteration == ITERS - 1:
-            row_feat = (img_unit.astype(jnp.float32) * row_scale[:1]).astype(jnp.bfloat16)
+            row_line = row_scale[...].T[:1]
+            row_feat = (img_unit.astype(jnp.float32) * row_line).astype(jnp.bfloat16)
             for pair in range(n // 2):
                 both = jnp.dot(
                     row_feat, kern[:, pair * LANES : (pair + 1) * LANES],
@@ -169,15 +178,14 @@
         arrived(1 + iteration, parts.at[iteration])
         col_sum = jnp.sum(parts[iteration], axis=0)
         scale[...] = mdl_mass_ref[...] / col_sum
-        col_wide = jnp.concatenate(
-            [jnp.broadcast_to(scale[line : line + 1, :], (REP, LANES)) for line in range(lines)], axis=1
-        )
-
-    weighted = (model[...].astype(jnp.float32) * col_wide[:1]).astype(jnp.bfloat16)
+        col_low = scale[...].astype(jnp.bfloat16).astype(jnp.float32)
+
+    col_line = jnp.concatenate([scale[line : line + 1, :] for line in range(lines)], axis=1)
+    weighted = (model[...].astype(jnp.float32) * col_line).astype(jnp.bfloat16)
     image_terms = lax.dot_general(
         weighted, kern[...], (((1,), (1,)), ((), ())), preferred_element_type=jnp.float32
     )
-    grad_img_ref[...] = -(image_terms * row_scale[:1])
+    grad_img_ref[...] = -(image_terms * row_line)
 
     feat_in[me] = feat_out[me]
     arrived(1 + ITERS, feat_in)
@@ -231,6 +239,8 @@
             pltpu.VMEM(packed, jnp.bfloat16),
             pltpu.VMEM((FEAT, total), jnp.bfloat16),
             pltpu.VMEM((rows, total), jnp.bfloat16),
+            pltpu.VMEM((rows, total), jnp.float32),
+            pltpu.VMEM((rows, LANES), jnp.float32),
             pltpu.VMEM((ITERS, n, lines, LANES), jnp.float32),
             pltpu.VMEM((lines, LANES), jnp.float32),
             pltpu.VMEM(packed, jnp.bfloat16),

time: 34.1 us -> 33.5 us (0.982)
  Pallas kernels: 33.2 us -> 32.6 us
    pallas_call x1, Pallas kernels: 32.5 us -> 31.9 us  [shards(): pl.pallas_call(functools.partial(whole_kernel, n), out_shape=(pltpu.VMEM(...]
where the time goes in v5:
time: 33.5 us; the launch traced here: 33.2 us
  Pallas kernels  32.6 us (97%)
  between operations  0.64 us (2%)
    pallas_call x1, Pallas kernels, shards(): pl.pallas_call(functools.partial(whole_kernel, n), out_shape=(pltpu.VMEM(...  31.9 us
    pallas_call x1, Pallas kernels, shards(): pl.pallas_call(store_kernel, out_shape=(jax.ShapeDtypeStruct((FEAT, rows)...  0.68 us

profile of v5, /device:TPU:0, one launch (start us, length us, event | category | flops | bytes accessed | tf_op | source)
XLA Modules:
  0.0 33.2 jit_solution(17069185619130703469)
XLA Ops:
  0.6 31.9 %sinkhorn.1 = (f32[64,512]{1,0:T(8,128)S(1)}, f32[64,64]{1,0:T(8,128)S(1)}) custom-call(bf16[64,512]{1,0:T(8,128)(2,1)} %img_hbm.1, bf16[64,64]{1,0:T(8,128)(2,1)} %mdl_hbm.1, f32[1,512]{1,0:T(1,128)} %bitcast.3, f32[8,128]{1,0:T(8,128)} %bitcast.2), custom_call_target="tpu_custom_call" | custom-call | tf_op jit(solution)/shard_map/sinkhorn/pallas_call | solution.py:226
  32.5 0.7 %store.1 = (f32[64,512]{1,0:T(8,128)}, f32[64,64]{1,0:T(8,128)}) custom-call(f32[64,512]{1,0:T(8,128)S(1)} %get-tuple-element.4.grad_img_ref, f32[64,64]{1,0:T(8,128)S(1)} %get-tuple-element.5.grad_mdl_ref), custom_call_target="tpu_custom_call" | custom-call | tf_op jit(solution)/shard_map/store/pallas_call | solution.py:258

commit v6 on v5

--- a/solution.py
+++ b/solution.py
@@ -159,7 +159,8 @@
             partial_cols += jnp.sum((wide[here] * row_low).reshape(block // 8, 8, total), axis=0)
         partial_cols = jnp.sum(partial_cols, axis=0, keepdims=True)
         for line in range(lines):
-            parts[iteration, me, line : line + 1, :] = partial_cols[:, line * LANES : (line + 1) * LANES]
+            scale[line : line + 1, :] = partial_cols[:, line * LANES : (line + 1) * LANES]
+        parts[iteration, me] = scale[...].astype(jnp.bfloat16)
         send(1 + iteration, lambda to: parts.at[iteration, me], parts.at[iteration, me], recv_sem.at[1 + iteration])
 
         if iteration == ITERS - 1:
@@ -176,7 +177,7 @@
             send(1 + ITERS, lambda to: feat_out.at[to], feat_in.at[me], recv_sem.at[1 + ITERS])
 
         arrived(1 + iteration, parts.at[iteration])
-        col_sum = jnp.sum(parts[iteration], axis=0)
+        col_sum = jnp.sum(parts[iteration].astype(jnp.float32), axis=0)
         scale[...] = mdl_mass_ref[...] / col_sum
         col_low = scale[...].astype(jnp.bfloat16).astype(jnp.float32)
 
@@ -241,7 +242,7 @@
             pltpu.VMEM((rows, total), jnp.bfloat16),
             pltpu.VMEM((rows, total), jnp.float32),
             pltpu.VMEM((rows, LANES), jnp.float32),
-            pltpu.VMEM((ITERS, n, lines, LANES), jnp.float32),
+            pltpu.VMEM((ITERS, n, lines, LANES), jnp.bfloat16),
             pltpu.VMEM((lines, LANES), jnp.float32),
             pltpu.VMEM(packed, jnp.bfloat16),
             pltpu.VMEM(packed, jnp.bfloat16),

time: 33.5 us -> 32.7 us (0.976)
  Pallas kernels: 32.6 us -> 31.9 us
    pallas_call x1, Pallas kernels: 31.9 us -> 31.2 us  [shards(): pl.pallas_call(functools.partial(whole_kernel, n), out_shape=(pltpu.VMEM(...]
where the time goes in v6:
time: 32.7 us; the launch traced here: 32.5 us
  Pallas kernels  31.9 us (98%)
  between operations  0.64 us (2%)
    pallas_call x1, Pallas kernels, shards(): pl.pallas_call(functools.partial(whole_kernel, n), out_shape=(pltpu.VMEM(...  31.2 us
    pallas_call x1, Pallas kernels, shards(): pl.pallas_call(store_kernel, out_shape=(jax.ShapeDtypeStruct((FEAT, rows)...  0.68 us

profile of v6, /device:TPU:0, one launch (start us, length us, event | category | flops | bytes accessed | tf_op | source)
XLA Modules:
  0.0 32.5 jit_solution(3364704810226514188)
XLA Ops:
  0.6 31.2 %sinkhorn.1 = (f32[64,512]{1,0:T(8,128)S(1)}, f32[64,64]{1,0:T(8,128)S(1)}) custom-call(bf16[64,512]{1,0:T(8,128)(2,1)} %img_hbm.1, bf16[64,64]{1,0:T(8,128)(2,1)} %mdl_hbm.1, f32[1,512]{1,0:T(1,128)} %bitcast.3, f32[8,128]{1,0:T(8,128)} %bitcast.2), custom_call_target="tpu_custom_call" | custom-call | tf_op jit(solution)/shard_map/sinkhorn/pallas_call | solution.py:227
  31.8 0.7 %store.1 = (f32[64,512]{1,0:T(8,128)}, f32[64,64]{1,0:T(8,128)}) custom-call(f32[64,512]{1,0:T(8,128)S(1)} %get-tuple-element.4.grad_img_ref, f32[64,64]{1,0:T(8,128)S(1)} %get-tuple-element.5.grad_mdl_ref), custom_call_target="tpu_custom_call" | custom-call | tf_op jit(solution)/shard_map/store/pallas_call | solution.py:259

commit v7 on v6

--- a/solution.py
+++ b/solution.py
@@ -49,8 +49,10 @@
     total = kern.shape[1]
     lines = total // LANES
 
+    partners = [other(me, n - 1 - step, n) for step in range(n - 1)] if n <= 16 else None
+
     def partner(step):
-        return other(me, n - 1 - step, n)
+        return partners[step] if partners else other(me, step + 1, n)
 
     def send(phase, source, target_slot, landed):
         def one(step, carry):
@@ -143,19 +145,20 @@
     row_sums = repeat(total // chunk, build, jnp.zeros((rows, LANES), jnp.float32))
 
     for iteration in range(ITERS):
+        partial_cols = jnp.zeros((8, total), jnp.float32)
         for start in range(0, rows, block):
             here = slice(start, start + block)
             if iteration == 0:
                 by_lane = row_sums[here]
             else:
-                by_lane = jnp.zeros((block, LANES), jnp.float32)
-                for line in range(lines):
-                    by_lane += wide[here, line * LANES : (line + 1) * LANES] * col_low[line : line + 1]
-            row_scale[here] = img_mass[here] / jnp.sum(by_lane, axis=1, keepdims=True)
-        partial_cols = jnp.zeros((8, total), jnp.float32)
-        for start in range(0, rows, block):
-            here = slice(start, start + block)
-            row_low = row_scale[here, :1].astype(jnp.bfloat16).astype(jnp.float32)
+                by_lane = wide[here, :LANES] * col_low[0]
+                for line in range(1, lines):
+                    by_lane += wide[here, line * LANES : (line + 1) * LANES] * col_low[line]
+            scaled = img_mass[here] / jnp.broadcast_to(jnp.sum(by_lane, axis=1, keepdims=True), (block, LANES))
+            if iteration == ITERS - 1:
+                row_scale[here] = scaled
+            row_low = scaled.astype(jnp.bfloat16).astype(jnp.float32)
+            row_low = jnp.concatenate([row_low] * lines, axis=1)
             partial_cols += jnp.sum((wide[here] * row_low).reshape(block // 8, 8, total), axis=0)
         partial_cols = jnp.sum(partial_cols, axis=0, keepdims=True)
         for line in range(lines):
@@ -166,20 +169,25 @@
         if iteration == ITERS - 1:
             row_line = row_scale[...].T[:1]
             row_feat = (img_unit.astype(jnp.float32) * row_line).astype(jnp.bfloat16)
-            for pair in range(n // 2):
-                both = jnp.dot(
-                    row_feat, kern[:, pair * LANES : (pair + 1) * LANES],
+            for quad in range(n // 4):
+                four = jnp.dot(
+                    row_feat, kern[:, quad * chunk : (quad + 1) * chunk],
                     preferred_element_type=jnp.float32,
                 )
-                top, bottom = both[: FEAT // 2], both[FEAT // 2 :]
-                feat_out[2 * pair] = jnp.where(left, top, pltpu.roll(bottom, HALF, 1)).astype(jnp.bfloat16)
-                feat_out[2 * pair + 1] = jnp.where(left, pltpu.roll(top, HALF, 1), bottom).astype(jnp.bfloat16)
+                for pair in range(2):
+                    both = four[:, pair * LANES : (pair + 1) * LANES]
+                    slot = 4 * quad + 2 * pair
+                    top, bottom = both[: FEAT // 2], both[FEAT // 2 :]
+                    feat_out[slot] = jnp.where(left, top, pltpu.roll(bottom, HALF, 1)).astype(jnp.bfloat16)
+                    feat_out[slot + 1] = jnp.where(left, pltpu.roll(top, HALF, 1), bottom).astype(jnp.bfloat16)
             send(1 + ITERS, lambda to: feat_out.at[to], feat_in.at[me], recv_sem.at[1 + ITERS])
 
         arrived(1 + iteration, parts.at[iteration])
         col_sum = jnp.sum(parts[iteration].astype(jnp.float32), axis=0)
         scale[...] = mdl_mass_ref[...] / col_sum
-        col_low = scale[...].astype(jnp.bfloat16).astype(jnp.float32)
+        if iteration < ITERS - 1:
+            low = scale[...].astype(jnp.bfloat16).astype(jnp.float32)
+            col_low = [jnp.broadcast_to(low[line : line + 1], (block, LANES)) for line in range(lines)]
 
     col_line = jnp.concatenate([scale[line : line + 1, :] for line in range(lines)], axis=1)
     weighted = (model[...].astype(jnp.float32) * col_line).astype(jnp.bfloat16)

time: 32.7 us -> 32.4 us (level)
  Pallas kernels: 31.9 us -> 31.5 us
    pallas_call x1, Pallas kernels: 31.2 us -> 30.8 us  [shards(): pl.pallas_call(functools.partial(whole_kernel, n), out_shape=(pltpu.VMEM(...]
where the time goes in v7:
time: 32.4 us; the launch traced here: 32.2 us
  Pallas kernels  31.5 us (97%)
  between operations  0.64 us (2%)
    pallas_call x1, Pallas kernels, shards(): pl.pallas_call(functools.partial(whole_kernel, n), out_shape=(pltpu.VMEM(...  30.8 us
    pallas_call x1, Pallas kernels, shards(): pl.pallas_call(store_kernel, out_shape=(jax.ShapeDtypeStruct((FEAT, rows)...  0.68 us

profile of v7, /device:TPU:0, one launch (start us, length us, event | category | flops | bytes accessed | tf_op | source)
XLA Modules:
  0.0 32.2 jit_solution(6866946962776653331)
XLA Ops:
  0.6 30.8 %sinkhorn.1 = (f32[64,512]{1,0:T(8,128)S(1)}, f32[64,64]{1,0:T(8,128)S(1)}) custom-call(bf16[64,512]{1,0:T(8,128)(2,1)} %img_hbm.1, bf16[64,64]{1,0:T(8,128)(2,1)} %mdl_hbm.1, f32[1,512]{1,0:T(1,128)} %bitcast.3, f32[8,128]{1,0:T(8,128)} %bitcast.2), custom_call_target="tpu_custom_call" | custom-call | tf_op jit(solution)/shard_map/sinkhorn/pallas_call | solution.py:235
  31.5 0.7 %store.1 = (f32[64,512]{1,0:T(8,128)}, f32[64,64]{1,0:T(8,128)}) custom-call(f32[64,512]{1,0:T(8,128)S(1)} %get-tuple-element.4.grad_img_ref, f32[64,64]{1,0:T(8,128)S(1)} %get-tuple-element.5.grad_mdl_ref), custom_call_target="tpu_custom_call" | custom-call | tf_op jit(solution)/shard_map/store/pallas_call | solution.py:267

commit v8 on v7

--- a/solution.py
+++ b/solution.py
@@ -114,7 +114,7 @@
     rows = kern.shape[0]
     block = 64
 
-    def build(step, row_sums):
+    def build(step, carry):
         which = other(me // group, step, n // group)
         for sub in range(group):
             sender = which * group + sub
@@ -136,27 +136,32 @@
         scores = jnp.dot(img_rows, columns, preferred_element_type=jnp.float32)
         tile = jnp.exp(scores * factor).astype(jnp.bfloat16)
         kern[:, where] = tile
-        tile = tile.astype(jnp.float32)
-        wide[:, where] = tile
-        for line in range(chunk // LANES):
-            row_sums += tile[:, line * LANES : (line + 1) * LANES]
-        return row_sums
-
-    row_sums = repeat(total // chunk, build, jnp.zeros((rows, LANES), jnp.float32))
-
-    for iteration in range(ITERS):
+        wide[:, where] = tile.astype(jnp.float32)
+        return carry
+
+    lax.fori_loop(0, total // chunk, build, 0)
+    scale[...] = jnp.ones((lines, LANES), jnp.float32)
+
+    def finish(iteration):
+        arrived(1 + iteration, parts.at[iteration])
+        col_sum = jnp.sum(parts[iteration].astype(jnp.float32), axis=0)
+        scale[...] = mdl_mass_ref[...] / col_sum
+
+    def iterate(iteration, carry):
+        @pl.when(iteration > 0)
+        def _():
+            finish(iteration - 1)
+
+        low = scale[...].astype(jnp.bfloat16).astype(jnp.float32)
+        col_low = [jnp.broadcast_to(low[line : line + 1], (block, LANES)) for line in range(lines)]
         partial_cols = jnp.zeros((8, total), jnp.float32)
         for start in range(0, rows, block):
             here = slice(start, start + block)
-            if iteration == 0:
-                by_lane = row_sums[here]
-            else:
-                by_lane = wide[here, :LANES] * col_low[0]
-                for line in range(1, lines):
-                    by_lane += wide[here, line * LANES : (line + 1) * LANES] * col_low[line]
+            by_lane = wide[here, :LANES] * col_low[0]
+            for line in range(1, lines):
+                by_lane += wide[here, line * LANES : (line + 1) * LANES] * col_low[line]
             scaled = img_mass[here] / jnp.broadcast_to(jnp.sum(by_lane, axis=1, keepdims=True), (block, LANES))
-            if iteration == ITERS - 1:
-                row_scale[here] = scaled
+            row_scale[here] = scaled
             row_low = scaled.astype(jnp.bfloat16).astype(jnp.float32)
             row_low = jnp.concatenate([row_low] * lines, axis=1)
             partial_cols += jnp.sum((wide[here] * row_low).reshape(block // 8, 8, total), axis=0)
@@ -164,31 +169,28 @@
         for line in range(lines):
             scale[line : line + 1, :] = partial_cols[:, line * LANES : (line + 1) * LANES]
         parts[iteration, me] = scale[...].astype(jnp.bfloat16)
-        send(1 + iteration, lambda to: parts.at[iteration, me], parts.at[iteration, me], recv_sem.at[1 + iteration])
-
-        if iteration == ITERS - 1:
-            row_line = row_scale[...].T[:1]
-            row_feat = (img_unit.astype(jnp.float32) * row_line).astype(jnp.bfloat16)
-            for quad in range(n // 4):
-                four = jnp.dot(
-                    row_feat, kern[:, quad * chunk : (quad + 1) * chunk],
-                    preferred_element_type=jnp.float32,
-                )
-                for pair in range(2):
-                    both = four[:, pair * LANES : (pair + 1) * LANES]
-                    slot = 4 * quad + 2 * pair
-                    top, bottom = both[: FEAT // 2], both[FEAT // 2 :]
-                    feat_out[slot] = jnp.where(left, top, pltpu.roll(bottom, HALF, 1)).astype(jnp.bfloat16)
-                    feat_out[slot + 1] = jnp.where(left, pltpu.roll(top, HALF, 1), bottom).astype(jnp.bfloat16)
-            send(1 + ITERS, lambda to: feat_out.at[to], feat_in.at[me], recv_sem.at[1 + ITERS])
-
-        arrived(1 + iteration, parts.at[iteration])
-        col_sum = jnp.sum(parts[iteration].astype(jnp.float32), axis=0)
-        scale[...] = mdl_mass_ref[...] / col_sum
-        if iteration < ITERS - 1:
-            low = scale[...].astype(jnp.bfloat16).astype(jnp.float32)
-            col_low = [jnp.broadcast_to(low[line : line + 1], (block, LANES)) for line in range(lines)]
-
+        mine = parts.at[iteration, me]
+        send(1 + iteration, lambda to: mine, mine, recv_sem.at[1 + iteration])
+        return carry
+
+    lax.fori_loop(0, ITERS, iterate, 0)
+
+    row_line = row_scale[...].T[:1]
+    row_feat = (img_unit.astype(jnp.float32) * row_line).astype(jnp.bfloat16)
+    for quad in range(n // 4):
+        four = jnp.dot(
+            row_feat, kern[:, quad * chunk : (quad + 1) * chunk],
+            preferred_element_type=jnp.float32,
+        )
+        for pair in range(2):
+            both = four[:, pair * LANES : (pair + 1) * LANES]
+            slot = 4 * quad + 2 * pair
+            top, bottom = both[: FEAT // 2], both[FEAT // 2 :]
+            feat_out[slot] = jnp.where(left, top, pltpu.roll(bottom, HALF, 1)).astype(jnp.bfloat16)
+            feat_out[slot + 1] = jnp.where(left, pltpu.roll(top, HALF, 1), bottom).astype(jnp.bfloat16)
+    send(1 + ITERS, lambda to: feat_out.at[to], feat_in.at[me], recv_sem.at[1 + ITERS])
+
+    finish(ITERS - 1)
     col_line = jnp.concatenate([scale[line : line + 1, :] for line in range(lines)], axis=1)
     weighted = (model[...].astype(jnp.float32) * col_line).astype(jnp.bfloat16)
     image_terms = lax.dot_general(

time: 32.4 us -> 32.5 us (level)
  no operation moved by 1% of the time
where the time goes in v8:
time: 32.5 us; the launch traced here: 32.3 us
  Pallas kernels  31.7 us (98%)
  between operations  0.64 us (2%)
    pallas_call x1, Pallas kernels, shards(): pl.pallas_call(functools.partial(whole_kernel, n), out_shape=(pltpu.VMEM(...  31 us
    pallas_call x1, Pallas kernels, shards(): pl.pallas_call(store_kernel, out_shape=(jax.ShapeDtypeStruct((FEAT, rows)...  0.68 us

profile of v8, /device:TPU:0, one launch (start us, length us, event | category | flops | bytes accessed | tf_op | source)
XLA Modules:
  0.0 32.3 jit_solution(7503005431772796330)
XLA Ops:
  0.6 31.0 %sinkhorn.1 = (f32[64,512]{1,0:T(8,128)S(1)}, f32[64,64]{1,0:T(8,128)S(1)}) custom-call(bf16[64,512]{1,0:T(8,128)(2,1)} %img_hbm.1, bf16[64,64]{1,0:T(8,128)(2,1)} %mdl_hbm.1, f32[1,512]{1,0:T(1,128)} %bitcast.3, f32[8,128]{1,0:T(8,128)} %bitcast.2), custom_call_target="tpu_custom_call" | custom-call | tf_op jit(solution)/shard_map/sinkhorn/pallas_call | solution.py:237
  31.6 0.7 %store.1 = (f32[64,512]{1,0:T(8,128)}, f32[64,64]{1,0:T(8,128)}) custom-call(f32[64,512]{1,0:T(8,128)S(1)} %get-tuple-element.4.grad_img_ref, f32[64,64]{1,0:T(8,128)S(1)} %get-tuple-element.5.grad_mdl_ref), custom_call_target="tpu_custom_call" | custom-call | tf_op jit(solution)/shard_map/store/pallas_call | solution.py:269

commit v9 on v8

--- a/solution.py
+++ b/solution.py
@@ -112,7 +112,7 @@
     chunk = 2 * LANES
     group = chunk // HALF
     rows = kern.shape[0]
-    block = 64
+    block = 16
 
     def build(step, carry):
         which = other(me // group, step, n // group)

time: 32.5 us -> 32.5 us (level)
  no operation moved by 1% of the time
where the time goes in v9:
time: 32.5 us; the launch traced here: 32.3 us
  Pallas kernels  31.7 us (98%)
  between operations  0.64 us (2%)
    pallas_call x1, Pallas kernels, shards(): pl.pallas_call(functools.partial(whole_kernel, n), out_shape=(pltpu.VMEM(...  31 us
    pallas_call x1, Pallas kernels, shards(): pl.pallas_call(store_kernel, out_shape=(jax.ShapeDtypeStruct((FEAT, rows)...  0.68 us

profile of v9, /device:TPU:0, one launch (start us, length us, event | category | flops | bytes accessed | tf_op | source)
XLA Modules:
  0.0 32.3 jit_solution(10556854474789471042)
XLA Ops:
  0.6 31.0 %sinkhorn.1 = (f32[64,512]{1,0:T(8,128)S(1)}, f32[64,64]{1,0:T(8,128)S(1)}) custom-call(bf16[64,512]{1,0:T(8,128)(2,1)} %img_hbm.1, bf16[64,64]{1,0:T(8,128)(2,1)} %mdl_hbm.1, f32[1,512]{1,0:T(1,128)} %bitcast.3, f32[8,128]{1,0:T(8,128)} %bitcast.2), custom_call_target="tpu_custom_call" | custom-call | tf_op jit(solution)/shard_map/sinkhorn/pallas_call | solution.py:237
  31.6 0.7 %store.1 = (f32[64,512]{1,0:T(8,128)}, f32[64,64]{1,0:T(8,128)}) custom-call(f32[64,512]{1,0:T(8,128)S(1)} %get-tuple-element.4.grad_img_ref, f32[64,64]{1,0:T(8,128)S(1)} %get-tuple-element.5.grad_mdl_ref), custom_call_target="tpu_custom_call" | custom-call | tf_op jit(solution)/shard_map/store/pallas_call | solution.py:269

commit v10 on v9

--- a/solution.py
+++ b/solution.py
@@ -91,9 +91,9 @@
             ((mdl_hbm, mdl_ref), (img_hbm, img_ref), (img_mass_hbm, img_mass_ref), (mdl_mass_hbm, mdl_mass_ref))
         )
     ]
+    repeat(n - 1, greet)
     for load in loads:
         load.start()
-    repeat(n - 1, greet)
     loads[0].wait()
 
     own = normalize(mdl_ref[...])
@@ -144,7 +144,7 @@
 
     def finish(iteration):
         arrived(1 + iteration, parts.at[iteration])
-        col_sum = jnp.sum(parts[iteration].astype(jnp.float32), axis=0)
+        col_sum = jnp.sum(parts[iteration], axis=0)
         scale[...] = mdl_mass_ref[...] / col_sum
 
     def iterate(iteration, carry):
@@ -167,8 +167,7 @@
             partial_cols += jnp.sum((wide[here] * row_low).reshape(block // 8, 8, total), axis=0)
         partial_cols = jnp.sum(partial_cols, axis=0, keepdims=True)
         for line in range(lines):
-            scale[line : line + 1, :] = partial_cols[:, line * LANES : (line + 1) * LANES]
-        parts[iteration, me] = scale[...].astype(jnp.bfloat16)
+            parts[iteration, me, line : line + 1, :] = partial_cols[:, line * LANES : (line + 1) * LANES]
         mine = parts.at[iteration, me]
         send(1 + iteration, lambda to: mine, mine, recv_sem.at[1 + iteration])
         return carry
@@ -252,7 +251,7 @@
             pltpu.VMEM((rows, total), jnp.bfloat16),
             pltpu.VMEM((rows, total), jnp.float32),
             pltpu.VMEM((rows, LANES), jnp.float32),
-            pltpu.VMEM((ITERS, n, lines, LANES), jnp.bfloat16),
+            pltpu.VMEM((ITERS, n, lines, LANES), jnp.float32),
             pltpu.VMEM((lines, LANES), jnp.float32),
             pltpu.VMEM(packed, jnp.bfloat16),
             pltpu.VMEM(packed, jnp.bfloat16),

time: 32.5 us -> 33.3 us (1.025)
  Pallas kernels: 31.7 us -> 32.4 us
    pallas_call x1, Pallas kernels: 31 us -> 31.7 us  [shards(): pl.pallas_call(functools.partial(whole_kernel, n), out_shape=(pltpu.VMEM(...]
where the time goes in v10:
time: 33.3 us; the launch traced here: 33 us
  Pallas kernels  32.4 us (97%)
  between operations  0.64 us (2%)
    pallas_call x1, Pallas kernels, shards(): pl.pallas_call(functools.partial(whole_kernel, n), out_shape=(pltpu.VMEM(...  31.7 us
    pallas_call x1, Pallas kernels, shards(): pl.pallas_call(store_kernel, out_shape=(jax.ShapeDtypeStruct((FEAT, rows)...  0.68 us

profile of v10, /device:TPU:0, one launch (start us, length us, event | category | flops | bytes accessed | tf_op | source)
XLA Modules:
  0.0 33.0 jit_solution(8942915208184645421)
XLA Ops:
  0.6 31.7 %sinkhorn.1 = (f32[64,512]{1,0:T(8,128)S(1)}, f32[64,64]{1,0:T(8,128)S(1)}) custom-call(bf16[64,512]{1,0:T(8,128)(2,1)} %img_hbm.1, bf16[64,64]{1,0:T(8,128)(2,1)} %mdl_hbm.1, f32[1,512]{1,0:T(1,128)} %bitcast.3, f32[8,128]{1,0:T(8,128)} %bitcast.2), custom_call_target="tpu_custom_call" | custom-call | tf_op jit(solution)/shard_map/sinkhorn/pallas_call | solution.py:236
  32.3 0.7 %store.1 = (f32[64,512]{1,0:T(8,128)}, f32[64,64]{1,0:T(8,128)}) custom-call(f32[64,512]{1,0:T(8,128)S(1)} %get-tuple-element.4.grad_img_ref, f32[64,64]{1,0:T(8,128)S(1)} %get-tuple-element.5.grad_mdl_ref), custom_call_target="tpu_custom_call" | custom-call | tf_op jit(solution)/shard_map/store/pallas_call | solution.py:268
